TPU v7x, 128 devices: a whole 4x4x4 slice. The times are simulated.
128 devices in a mesh: row: 16 (over z, y), col: 8 (over x, core).
Axes of the slice: x: 4, y: 4, z: 4, core: 2. Of those that a mesh axis runs over, the one named last changes fastest.
Arguments:
- panel_blocks: bfloat16 [8192, 2048], P('row', 'col'), may hold values from -4 to 4
- live_rows: int32 [8, 32], P('col', 'row'), may hold values from 0 to 2, as said below
- window_blocks: bfloat16 [2048, 2048], P(None, 'col'), as said below
- diag_inverse: bfloat16 [8, 256, 256], P('col'), as said below
- trailing: float32 [8192, 8192], P('row', 'col'), may hold values from -6 to 6
Outputs:
- panel_factor: bfloat16 [8192, 2048], P('row', 'col')
- window_factor: bfloat16 [2048, 2048], P(None, 'col')
- trailing_out: float32 [8192, 8192], P('row', 'col')
Inputs may be any that keep to these rules, and one draw needn't show every extreme that they name: `live_rows`: for each panel and row index the 2 entries are distinct local block rows in ascending order followed by 2 for empty slots; each row index has at least one live slot per panel; in every panel some row index has all 2 slots live and some other row index has an empty slot. `diag_inverse`: each matrix is lower triangular with a positive diagonal. `window_blocks`: entries lie within plus or minus 24 / sqrt(256).
All inputs are finite; a program needn't handle non-finite values.
Results may differ from a plain program's by a relative error of at most 0.009.
Values may be sent and summed in bfloat16 or wider, within the bound.
A program may use at most 128 MiB of HBM per device.

v0:
```python
import jax
import jax.numpy as jnp
from jax import lax
from jax.sharding import PartitionSpec as P


def broadcast(value, axis, root):
    mine = lax.axis_index(axis) == root
    return lax.psum(jnp.where(mine, value, jnp.zeros_like(value)), axis)


def expand(slot_data, slot_rows, count):
    width = slot_data.shape[1]
    onehot = (slot_rows[0][:, None] == jnp.arange(count)[None, :]).astype(jnp.bfloat16)
    spread = jnp.einsum(
        "si,sab->iab",
        onehot,
        slot_data.reshape(-1, width, width),
        preferred_element_type=jnp.float32,
    )
    return spread.astype(jnp.bfloat16).reshape(count * width, width)


def select_rows(full_rows, slot_rows):
    width = full_rows.shape[1]
    count = full_rows.shape[0] // width
    onehot = (slot_rows[0][:, None] == jnp.arange(count)[None, :]).astype(jnp.bfloat16)
    picked = jnp.einsum(
        "si,iab->sab",
        onehot,
        full_rows.reshape(count, width, width),
        preferred_element_type=jnp.float32,
    )
    return picked.astype(jnp.bfloat16).reshape(-1, width)


def local(panel_blocks, live_rows, window_blocks, diag_inverse, trailing):
    width = diag_inverse.shape[-1]
    row_blocks = trailing.shape[0] // width
    col_blocks = trailing.shape[1] // width
    panel_count = window_blocks.shape[0] // width
    roots = col_blocks // row_blocks
    column = lax.axis_index("col")
    inverse = diag_inverse[0]
    slot_keep = jnp.repeat(live_rows[0] < row_blocks, width)[:, None]
    lanes = jnp.arange(panel_count * width) // width
    acc_panel = panel_blocks.astype(jnp.float32)
    acc_window = window_blocks.astype(jnp.float32)
    trail = trailing
    mine_panel = jnp.zeros(panel_blocks.shape, jnp.bfloat16)
    mine_window = jnp.zeros(window_blocks.shape, jnp.bfloat16)
    for p in range(panel_count):

        def solve_here():
            solved = jnp.dot(
                acc_panel.astype(jnp.bfloat16), inverse.T, preferred_element_type=jnp.float32
            )
            solved = jnp.where(slot_keep, solved, 0.0).astype(jnp.bfloat16)
            solved_w = jnp.dot(
                acc_window.astype(jnp.bfloat16), inverse.T, preferred_element_type=jnp.float32
            )
            solved_w = jnp.where((lanes > p)[:, None], solved_w, 0.0).astype(jnp.bfloat16)
            return (solved, solved_w)

        def nothing():
            return (
                jnp.zeros(panel_blocks.shape, jnp.bfloat16),
                jnp.zeros(window_blocks.shape, jnp.bfloat16),
            )

        factor_slots, factor_window = lax.cond(column == p, solve_here, nothing)
        mine_panel = mine_panel + factor_slots
        mine_window = mine_window + factor_window
        start = min(p + 1, panel_count - 1)
        window_send = factor_window[start * width :]
        full_rows = expand(factor_slots, live_rows, row_blocks)
        rows_here, window_here = (broadcast(full_rows, "col", p), broadcast(window_send, "col", p))
        pieces = []
        for m in range(roots):
            pieces.append(broadcast(rows_here, "row", column * roots + m))
        column_rows = jnp.concatenate(pieces, axis=0)
        later = column > p
        offset = jnp.clip(column - start, 0, window_here.shape[0] // width - 1)
        w_block = lax.dynamic_slice_in_dim(window_here, offset * width, width, 0)
        picked = select_rows(rows_here, live_rows)
        acc_panel = acc_panel - jnp.where(
            later, jnp.dot(picked, w_block.T, preferred_element_type=jnp.float32), 0.0
        )
        lower_part = jnp.where(
            later, jnp.dot(window_here, w_block.T, preferred_element_type=jnp.float32), 0.0
        )
        acc_window = acc_window.at[start * width :].add(-lower_part)
        trail = trail - jnp.dot(rows_here, column_rows.T, preferred_element_type=jnp.float32)
    return (mine_panel, mine_window, trail)


def solution(mesh):
    return jax.shard_map(
        local,
        mesh=mesh,
        in_specs=(
            P("row", "col"),
            P("col", "row"),
            P(None, "col"),
            P("col", None, None),
            P("row", "col"),
        ),
        out_specs=(P("row", "col"), P(None, "col"), P("row", "col")),
        check_vma=False,
    )
```

profile of v0, /device:TPU:1, one launch (start us, length us, event | category | flops | bytes accessed | tf_op | source)
XLA Modules:
  0.0 698.3 jit_solution(1144228948789417028)
XLA Ops:
  9.4 2.0 conditional.8
  13.7 65.7 %all-reduce.34.cloned.1.call-done = (bf16[512,256]{1,0:T(8,128)(2,1)}, bf16[1792,256]{1,0:T(8,128)(2,1)}) async-done(((bf16[512,256]{1,0:T(8,128)(2,1)}, bf16[1792,256]{1,0:T(8,128)(2,1)}), (bf16[512,256]{1,0:T(8,128)(2,1)}, bf16[1792,256]{1,0:T(8,128)(2,1)})) %all-reduce.34.cloned.1.call-update) | async-done | bytes 1179664 | tf_op jit(solution)/shard_map/psum | solution.py:9
  79.3 1.5 convolution_convert_fusion.13
  82.6 3.7 conditional.9
  89.4 60.0 %all-reduce.32.cloned.1.call-done = (bf16[512,256]{1,0:T(8,128)(2,1)}, bf16[1536,256]{1,0:T(8,128)(2,1)}) async-done(((bf16[512,256]{1,0:T(8,128)(2,1)}, bf16[1536,256]{1,0:T(8,128)(2,1)}), (bf16[512,256]{1,0:T(8,128)(2,1)}, bf16[1536,256]{1,0:T(8,128)(2,1)})) %all-reduce.32.cloned.1.call-update) | async-done | bytes 1048592 | tf_op jit(solution)/shard_map/psum | solution.py:9
  149.5 1.5 convolution_convert_fusion.11
  151.1 3.0 constant_dynamic-update-slice_fusion.4
  154.4 2.0 conditional.10
  158.5 62.5 %all-reduce.30.cloned.1.call-done = (bf16[512,256]{1,0:T(8,128)(2,1)}, bf16[1280,256]{1,0:T(8,128)(2,1)}) async-done(((bf16[512,256]{1,0:T(8,128)(2,1)}, bf16[1280,256]{1,0:T(8,128)(2,1)}), (bf16[512,256]{1,0:T(8,128)(2,1)}, bf16[1280,256]{1,0:T(8,128)(2,1)})) %all-reduce.30.cloned.1.call-update) | async-done | bytes 917520 | tf_op jit(solution)/shard_map/psum | solution.py:9
  220.9 1.6 convolution_convert_fusion.9
  225.2 1.9 conditional.11
  230.2 1.8 broadcast_select_fusion.20
  232.0 59.1 %all-reduce.28.cloned.1.call-done = (bf16[512,256]{1,0:T(8,128)(2,1)}, bf16[1024,256]{1,0:T(8,128)(2,1)}) async-done(((bf16[512,256]{1,0:T(8,128)(2,1)}, bf16[1024,256]{1,0:T(8,128)(2,1)}), (bf16[512,256]{1,0:T(8,128)(2,1)}, bf16[1024,256]{1,0:T(8,128)(2,1)})) %all-reduce.28.cloned.1.call-update) | async-done | bytes 786448 | tf_op jit(solution)/shard_map/psum | solution.py:9
  291.1 1.6 convolution_convert_fusion.7
  295.3 1.8 conditional.12
  300.2 1.8 broadcast_select_fusion.19
  302.0 1.8 broadcast_select_fusion.18
  303.8 56.8 %all-reduce.26.cloned.1.call-done = (bf16[512,256]{1,0:T(8,128)(2,1)}, bf16[768,256]{1,0:T(8,128)(2,1)}) async-done(((bf16[512,256]{1,0:T(8,128)(2,1)}, bf16[768,256]{1,0:T(8,128)(2,1)}), (bf16[512,256]{1,0:T(8,128)(2,1)}, bf16[768,256]{1,0:T(8,128)(2,1)})) %all-reduce.26.cloned.1.call-update) | async-done | bytes 655376 | tf_op jit(solution)/shard_map/psum | solution.py:9
  360.6 1.6 convolution_convert_fusion.5
  369.6 59.4 %all-reduce.24.cloned.1.call-done = (bf16[512,256]{1,0:T(8,128)(2,1)}, bf16[512,256]{1,0:T(8,128)(2,1)}) async-done(((bf16[512,256]{1,0:T(8,128)(2,1)}, bf16[512,256]{1,0:T(8,128)(2,1)}), (bf16[512,256]{1,0:T(8,128)(2,1)}, bf16[512,256]{1,0:T(8,128)(2,1)})) %all-reduce.24.cloned.1.call-update) | async-done | bytes 524304 | tf_op jit(solution)/shard_map/psum | solution.py:9
  431.7 2.1 constant_dynamic-update-slice_fusion
  433.8 1.8 conditional.14
  438.5 60.8 %all-reduce.22.cloned.1.call-done = (bf16[512,256]{1,0:T(8,128)(2,1)}, bf16[256,256]{1,0:T(8,128)(2,1)}) async-done(((bf16[512,256]{1,0:T(8,128)(2,1)}, bf16[256,256]{1,0:T(8,128)(2,1)}), (bf16[512,256]{1,0:T(8,128)(2,1)}, bf16[256,256]{1,0:T(8,128)(2,1)})) %all-reduce.22.cloned.1.call-update) | async-done | bytes 393232 | tf_op jit(solution)/shard_map/psum | solution.py:9
  500.8 1.9 fusion.139
  503.8 1.8 conditional.15
  508.7 59.1 %all-reduce.18.cloned.1.call-done = bf16[512,256]{1,0:T(8,128)(2,1)} async-done(((bf16[512,256]{1,0:T(8,128)(2,1)}), bf16[512,256]{1,0:T(8,128)(2,1)}) %all-reduce.18.cloned.1.call-update) | async-done | bytes 262160 | tf_op jit(solution)/shard_map/psum | solution.py:9
  567.8 1.8 broadcast_select_fusion.13
  570.6 2.1 add_add_fusion.1
  572.7 4.7 add_add_fusion
  577.4 104.8 %all-reduce.20.cloned.1.call-done = (bf16[512,256]{1,0:T(8,128)(2,1)}, bf16[512,256]{1,0:T(8,128)(2,1)}, bf16[512,256]{1,0:T(8,128)(2,1)}, bf16[512,256]{1,0:T(8...) async-done(((bf16[512,256]{1,0:T(8,128)(2,1)}, ...) | async-done | bytes 4194320 | tf_op jit(solution)/shard_map/psum | solution.py:9
  682.2 1.6 fusion.82
  689.4 2.4 subtract_subtract_fusion
  (199 shorter events, 63.7 us)
Async XLA Ops:
  7.2 2.2 copy-start
  7.2 72.1 %all-reduce.34.cloned.1.call-start = ((), (), s32[]{:S(2)}) async-start(), calls=%async_computation.8 | async-start | bytes 2359296 | tf_op jit(solution)/shard_map/psum | solution.py:9
  9.4 2.0 copy-start.48
  13.6 135.9 %all-reduce.32.cloned.1.call-start = ((), (), s32[]{:S(2)}) async-start(), calls=%async_computation.7 | async-start | bytes 2097152 | tf_op jit(solution)/shard_map/psum | solution.py:9
  89.4 131.6 %all-reduce.30.cloned.1.call-start = ((), (), s32[]{:S(2)}) async-start(), calls=%async_computation.6 | async-start | bytes 1835008 | tf_op jit(solution)/shard_map/psum | solution.py:9
  158.4 132.7 %all-reduce.28.cloned.1.call-start = ((), (), s32[]{:S(2)}) async-start(), calls=%async_computation.5 | async-start | bytes 1572864 | tf_op jit(solution)/shard_map/psum | solution.py:9
  220.9 2.8 copy-start.2
  220.9 2.9 copy-start.29
  230.1 130.6 %all-reduce.26.cloned.1.call-start = ((), (), s32[]{:S(2)}) async-start(), calls=%async_computation.4 | async-start | bytes 1310720 | tf_op jit(solution)/shard_map/psum | solution.py:9
  291.1 2.8 copy-start.5
  291.1 2.8 copy-start.30
  300.0 128.9 %all-reduce.24.cloned.1.call-start = ((), (), s32[]{:S(2)}) async-start(), calls=%async_computation.3 | async-start | bytes 1048576 | tf_op jit(solution)/shard_map/psum | solution.py:9
  360.6 2.8 copy-start.6
  360.6 2.8 copy-start.31
  365.8 2.1 copy-start.22
  365.8 2.9 copy-start.24
  367.1 63.4 %copy-start.4 = (f32[512,256]{1,0:T(8,128)S(1)}, f32[512,256]{1,0:T(8,128)}, u32[]{:S(2)}) copy-start(f32[512,256]{1,0:T(8,128)} %copy-done.3) | copy-start | bytes 1572868
  367.8 131.4 %all-reduce.22.cloned.1.call-start = ((), (), s32[]{:S(2)}) async-start(), calls=%async_computation.2 | async-start | bytes 786432 | tf_op jit(solution)/shard_map/psum | solution.py:9
  428.9 2.7 copy-start.32
  435.6 2.9 copy-start.15
  435.6 1.9 copy-start.26
  437.5 130.3 %all-reduce.18.cloned.1.call-start = ((), (), s32[]{:S(2)}) async-start(), calls=%async_computation | async-start | bytes 524288 | tf_op jit(solution)/shard_map/psum | solution.py:9
  499.2 3.5 copy-start.10
  505.6 2.3 copy-start.28
  507.8 174.4 %all-reduce.20.cloned.1.call-start = ((), (), s32[]{:S(2)}) async-start(), calls=%async_computation.1 | async-start | bytes 8388608 | tf_op jit(solution)/shard_map/psum | solution.py:9
  577.4 106.4 %copy-start.27 = (bf16[512,256]{1,0:T(8,128)(2,1)S(1)}, bf16[512,256]{1,0:T(8,128)(2,1)}, u32[]{:S(2)}) copy-start(bf16[512,256]{1,0:T(8,128)(2,1)} %get-tuple-element.373) | copy-start | bytes 786436
  682.2 1.6 copy-start.46
  682.2 1.6 copy-start.47
  687.6 1.7 copy-start.7
  687.6 1.6 copy-start.12
  687.6 1.7 copy-start.33
  687.6 1.8 copy-start.34
  (24 other events, 27.1 us)
Sparse Core Ops, SparseCore 0:
  13.7 65.5 all-reduce.33
  89.5 59.9 all-reduce.31
  158.5 62.3 all-reduce.29
  230.2 60.8 all-reduce.27
  300.1 60.4 all-reduce.25
  368.0 60.9 all-reduce.23
  437.6 61.5 all-reduce.21
  507.9 59.7 all-reduce.17
  573.8 108.3 all-reduce.19
where the time goes:
time: 699 us; the launch traced here: 698 us
  waiting for transfers between devices  588 us (84%)
  matrix products  44.4 us (6%)
  other arithmetic  25.3 us (4%)
  local copies, waits for them, and re-layouts  25.1 us (4%)
  between operations  14.6 us (2%)
    psum x9, waiting for transfers between devices, broadcast(): return lax.psum(jnp.where(mine, value, jnp.zeros_like(value)), axis)  588 us
    select_n x15, other arithmetic, broadcast(): return lax.psum(jnp.where(mine, value, jnp.zeros_like(value)), axis)  16.4 us
  transfers between devices with their start and end apart: 9, of which 9 were waited for; matrix products, arithmetic and copies ran while one was open for 2% of the time, Pallas kernels for 0%

commit v1 on v0

v1 whole, which is shorter than its diff:
```python
import functools

import jax
import jax.numpy as jnp
from jax import lax
from jax.experimental import pallas as pl
from jax.experimental.pallas import tpu as pltpu
from jax.sharding import PartitionSpec as P

B = 256
S = 16
N = 8
BF = jnp.bfloat16
F32 = jnp.float32
MESH = pl.DeviceIdType.MESH


def place():
    row = lax.axis_index("row")
    col = lax.axis_index("col")
    return row, col, col // 2, row % 4, row // 4, col % 2


def bits_of(y, z):
    return [((y + 1) // 2) % 2, ((z + 1) // 2) % 2, y // 2, z // 2]


def address(bits, k):
    return sum(bits[(k + i) % 4] * 2**i for i in range(4))


def partners(y, z):
    ya = y + 1 - 2 * (y % 2)
    za = z + 1 - 2 * (z % 2)
    return [z * 4 + ya, za * 4 + y, z * 4 + 3 - y, (3 - z) * 4 + y]


def gather_kernel(
    win, inv, pan, wg, arow, acol,
    wx_recv, wx_send, wh_recv, wh_send, wd_recv, wd_send,
    as_recv, as_send, ah_recv, ah_send, ar_recv, ar_send, lsem,
):
    row, col, x, y, z, core = place()
    bits = bits_of(y, z)
    addr = [address(bits, k) for k in range(4)]
    other = 1 - core

    def pick(a, b, c):
        return a * (1 - c) + b * c

    def remote(src, dst, ssem, rsem, r, c):
        return pltpu.make_async_remote_copy(
            src_ref=src, dst_ref=dst, send_sem=ssem, recv_sem=rsem, device_id=(r, c), device_id_type=MESH
        )

    def lanes(c):
        return pl.ds(pl.multiple_of(c * B, B), B)

    def rows(start, count):
        return pl.ds(pl.multiple_of(start, S), count)

    for j in range(4):

        @pl.when(x <= j)
        def _():
            for kc in range(2):
                q = 2 * j + kc
                t = addr[j] if kc == 0 else addr[3 - j]
                dst = wg.at[rows(q * B + t * S, S), lanes(col)]

                def send(src):
                    for d in range(4):
                        target = (x + d) % 4 * 2 + kc
                        if d == 0:

                            @pl.when(core == kc)
                            def _():
                                pltpu.make_async_copy(src, dst, wx_recv.at[j]).start()

                            @pl.when(core != kc)
                            def _():
                                remote(src, dst, wx_send.at[j], wx_recv.at[j], row, target).start()
                        else:
                            remote(src, dst, wx_send.at[j], wx_recv.at[j], row, target).start()

                @pl.when(q == col)
                def _():
                    send(inv.at[rows(t * S, S), :])

                @pl.when(q != col)
                def _():
                    send(win.at[rows(q * B + t * S, S), :])

    h = y % 2

    def scatter(t, carry):
        ty, tz = t % 4, t // 4
        tbits = bits_of(ty, tz)
        tcol = 2 * z + y // 2
        mine = (t == row) & (tcol == col)
        for kk in range(2):
            s = pick(address(tbits, kk), address(tbits, 2 + kk), h)
            src = pan.at[rows(kk * B + s * S, S), :]
            k = 2 * h + kk
            dst = acol.at[rows(k * B + s * S, S), lanes(col)]

            @pl.when(mine)
            def _():
                pltpu.make_async_copy(src, dst, as_recv.at[k]).start()

            @pl.when(jnp.logical_not(mine))
            def _():
                remote(src, dst, as_send, as_recv.at[k], t, tcol).start()

        return carry

    lax.fori_loop(0, 16, scatter, 0)

    dst = arow.at[:, lanes(col)]
    pltpu.make_async_copy(pan, dst, lsem).start()
    for d in range(1, 4):
        remote(pan, dst, ar_send.at[d - 1], ar_recv.at[col], row, (x + d) % 4 * 2 + core).start()
    remote(pan, dst, ar_send.at[3], ar_recv.at[col], row, x * 2 + other).start()

    near = partners(y, z)
    for i in range(4):
        n = 2**i
        for j in range(4):
            k_addr = pick(addr[j], addr[3 - j], core)
            q = 2 * j + core
            width = B * (2 * j + 2)
            if i == 0:
                got = wg.at[rows(q * B + k_addr * S, S), pl.ds(0, width)]
                pltpu.make_async_copy(got, got, wx_recv.at[j]).wait()
            else:
                m = n // 2
                base = k_addr // n * n + (1 - k_addr // m % 2) * m
                got = wg.at[rows(q * B + base * S, m * S), pl.ds(0, width)]
                pltpu.make_async_copy(got, got, wh_recv.at[i - 1, j]).wait()
            base = k_addr // n * n
            part = wg.at[rows(q * B + base * S, n * S), pl.ds(0, width)]
            to = pick(near[(j + i) % 4], near[(3 - j + i) % 4], core)
            remote(part, part, wh_send.at[i, j], wh_recv.at[i, j], to, col).start()
        for k in range(4):
            if i == 0:
                got = acol.at[rows(k * B + addr[k] * S, S), :]
                pltpu.make_async_copy(got, got, as_recv.at[k]).wait()
            else:
                m = n // 2
                base = addr[k] // n * n + (1 - addr[k] // m % 2) * m
                got = acol.at[rows(k * B + base * S, m * S), :]
                pltpu.make_async_copy(got, got, ah_recv.at[i - 1, k]).wait()
            base = addr[k] // n * n
            part = acol.at[rows(k * B + base * S, n * S), :]
            remote(part, part, ah_send.at[i, k], ah_recv.at[i, k], near[(k + i) % 4], col).start()

    for d in range(1, 4):
        c = (x + 4 - d) % 4 * 2 + core
        got = arow.at[:, lanes(c)]
        pltpu.make_async_copy(got, got, ar_recv.at[c]).wait()
        remote(got, got, ar_send.at[3 + d], ar_recv.at[c], row, x * 2 + other).start()
    for j in range(4):
        k_addr = pick(addr[j], addr[3 - j], core)
        q = 2 * j + core
        width = B * (2 * j + 2)
        base = (1 - k_addr // 8) * 8
        got = wg.at[rows(q * B + base * S, 8 * S), pl.ds(0, width)]
        pltpu.make_async_copy(got, got, wh_recv.at[3, j]).wait()
        part = wg.at[rows(q * B, B), pl.ds(0, width)]
        remote(part, part, wd_send.at[j], wd_recv.at[j], row, x * 2 + other).start()

    for k in range(4):
        base = (1 - addr[k] // 8) * 8
        got = acol.at[rows(k * B + base * S, 8 * S), :]
        pltpu.make_async_copy(got, got, ah_recv.at[3, k]).wait()
    for j in range(4):
        width = B * (2 * j + 2)
        got = wg.at[rows((2 * j + other) * B, B), pl.ds(0, width)]
        pltpu.make_async_copy(got, got, wd_recv.at[j]).wait()
        part = wg.at[rows((2 * j + core) * B, B), pl.ds(0, width)]
        pltpu.make_async_copy(part, part, wd_send.at[j]).wait()

        @pl.when(x <= j)
        def _():
            sent = pan.at[pl.ds(0, 7 * S), :]
            pltpu.make_async_copy(sent, sent, wx_send.at[j]).wait()

    for d in range(4):
        c = (x + d) % 4 * 2 + other
        got = arow.at[:, lanes(c)]
        pltpu.make_async_copy(got, got, ar_recv.at[c]).wait()
    pltpu.make_async_copy(pan, arow.at[:, lanes(col)], lsem).wait()
    for d in range(7):
        pltpu.make_async_copy(pan, pan, ar_send.at[d]).wait()
    own = (z == x) & (y // 2 == core)

    @pl.when(own)
    def _():
        sent = pan.at[pl.ds(0, 30 * S), :]
        pltpu.make_async_copy(sent, sent, as_send).wait()

    @pl.when(jnp.logical_not(own))
    def _():
        pltpu.make_async_copy(pan, pan, as_send).wait()

    for i in range(4):
        n = 2**i
        for j in range(4):
            k_addr = pick(addr[j], addr[3 - j], core)
            q = 2 * j + core
            width = B * (2 * j + 2)
            part = wg.at[rows(q * B + k_addr // n * n * S, n * S), pl.ds(0, width)]
            pltpu.make_async_copy(part, part, wh_send.at[i, j]).wait()
            part = acol.at[rows(j * B + addr[j] // n * n * S, n * S), :]
            pltpu.make_async_copy(part, part, ah_send.at[i, j]).wait()


def gather(win, inv, pan):
    dma = pltpu.SemaphoreType.DMA
    anys = pl.BlockSpec(memory_space=pl.ANY)
    return pl.pallas_call(
        gather_kernel,
        out_shape=(
            jax.ShapeDtypeStruct((N * B, N * B), BF),
            jax.ShapeDtypeStruct((2 * B, N * B), BF),
            jax.ShapeDtypeStruct((4 * B, N * B), BF),
        ),
        in_specs=[anys] * 3,
        out_specs=(anys,) * 3,
        scratch_shapes=[
            dma((4,)), dma((4,)), dma((4, 4)), dma((4, 4)), dma((4,)), dma((4,)),
            dma((4,)), dma(()), dma((4, 4)), dma((4, 4)), dma((8,)), dma((7,)), dma(()),
        ],
        compiler_params=pltpu.CompilerParams(has_side_effects=True),
        name="gather",
    )(win, inv, pan)


def nt(a, b):
    return lax.dot_general(a, b, (((1,), (1,)), ((), ())), preferred_element_type=F32)


def factor_kernel(live, at, wg, arow, acol, trail, pan_out, win_out, trail_out, wf, frow, fcol):
    row, col = at[0], at[1]

    def lane(p):
        return slice(p * B, p * B + B)

    for p in range(N):
        inv = wg[p * B : (p + 1) * B, lane(p)]
        prev = slice(0, p * B)

        def solve(raw, factors, ref_rows):
            acc = raw.astype(F32)
            if p > 0:
                acc = acc - nt(factors[ref_rows, prev], wf[p * B : (p + 1) * B, prev])
            return nt(acc.astype(BF), inv)

        def window_tile(q, carry):
            at_rows = pl.ds(pl.multiple_of(q * B, B), B)
            wf[at_rows, lane(p)] = solve(wg[at_rows, lane(p)], wf, at_rows).astype(BF)
            return carry

        lax.fori_loop(p + 1, N, window_tile, 0)

        def slots(src, dst, r, first):
            l0 = live[p, 2 * r]
            l1 = live[p, 2 * r + 1]
            for i in range(2):
                at_rows = slice(first + i * B, first + i * B + B)
                if i == 0:
                    raw = src[at_rows, lane(p)]
                    keep = l0 == 0
                else:
                    raw = jnp.where(l0 == 1, src[first : first + B, lane(p)], src[at_rows, lane(p)])
                    keep = (l0 == 1) | (l1 == 1)
                out = jnp.where(keep, solve(raw, dst, at_rows), 0.0)
                dst[at_rows, lane(p)] = out.astype(BF)

        slots(arow, frow, row, 0)
        for s in range(2):
            slots(acol, fcol, 2 * col + s, s * 2 * B)

    mine = pl.ds(pl.multiple_of(col * B, B), B)
    for q in range(N):
        block = wf[q * B : (q + 1) * B, mine]
        win_out[q * B : (q + 1) * B, :] = jnp.where(q > col, block, jnp.zeros_like(block))
    l0 = live[col, 2 * row]
    l1 = live[col, 2 * row + 1]
    f0 = frow[0:B, mine]
    f1 = frow[B : 2 * B, mine]
    pan_out[0:B, :] = jnp.where(l0 == 0, f0, f1)
    pan_out[B : 2 * B, :] = jnp.where(l1 == 1, f1, jnp.zeros_like(f1))
    for k in range(4):
        here = slice(k * B, k * B + B)
        trail_out[:, here] = trail[:, here] - nt(frow[...], fcol[here, :])


def factor(live, at, wg, arow, acol, trail):
    vmem = pl.BlockSpec(memory_space=pltpu.VMEM)
    smem = pl.BlockSpec(memory_space=pltpu.SMEM)
    return pl.pallas_call(
        factor_kernel,
        out_shape=(
            jax.ShapeDtypeStruct((2 * B, B), BF),
            jax.ShapeDtypeStruct((N * B, B), BF),
            jax.ShapeDtypeStruct(trail.shape, F32),
        ),
        in_specs=[smem, smem, vmem, vmem, vmem, vmem],
        out_specs=(vmem,) * 3,
        scratch_shapes=[
            pltpu.VMEM((N * B, N * B), BF),
            pltpu.VMEM((2 * B, N * B), BF),
            pltpu.VMEM((4 * B, N * B), BF),
        ],
        compiler_params=pltpu.CompilerParams(vmem_limit_bytes=56 * 2**20),
        name="factor",
    )(live, at, wg, arow, acol, trail)


def local(panel_blocks, live_rows, window_blocks, diag_inverse, trailing):
    live = lax.all_gather(live_rows, "row", axis=1, tiled=True)
    live = lax.all_gather(live, "col", axis=0, tiled=True)
    at = jnp.stack([lax.axis_index("row"), lax.axis_index("col")]).astype(jnp.int32)
    wg, arow, acol = gather(window_blocks, diag_inverse[0], panel_blocks)
    return factor(live, at, wg, arow, acol, trailing)


def solution(mesh):
    return jax.shard_map(
        local,
        mesh=mesh,
        in_specs=(
            P("row", "col"),
            P("col", "row"),
            P(None, "col"),
            P("col", None, None),
            P("row", "col"),
        ),
        out_specs=(P("row", "col"), P(None, "col"), P("row", "col")),
        check_vma=False,
    )
```

time: 699 us -> 136 us (0.19)
  the two profiles are of different devices: /device:TPU:1 before, /device:TPU:7 now
where the time goes in v1:
time: 136 us; the launch traced here: 135 us
  Pallas kernels  106 us (78%)
  blocking collectives  25.7 us (19%)
  local copies, waits for them, and re-layouts  1.99 us (1%)
    pallas_call x1, Pallas kernels, gather(): pl.pallas_call(gather_kernel, out_shape=(jax.ShapeDtypeStruct((N * B, N *...  67.8 us
    pallas_call x1, Pallas kernels, factor(): pl.pallas_call(factor_kernel, out_shape=(jax.ShapeDtypeStruct((2 * B, B),...  37.9 us
    unnamed x1, blocking collectives  14 us
    all_gather x1, blocking collectives, local(): live = lax.all_gather(live, 'col', axis=0, tiled=True)  11.7 us

profile of v1, /device:TPU:7, one launch (start us, length us, event | category | flops | bytes accessed | tf_op | source)
XLA Modules:
  0.0 135.4 jit_solution(16439087540724353684)
XLA Ops:
  0.6 0.7 pad_add_fusion.at
  1.3 1.2 dynamic-slice
  3.2 0.8 bitcast_dynamic-update-slice_fusion
  4.0 14.0 %all-reduce = s32[32]{0:T(128)S(1)} all-reduce(s32[32]{0:T(128)S(1)} %bitcast_dynamic-update-slice_fusion), channel_id=1, replica_groups=mesh['row'=16,'col'=8] {'row'}, use_global_device_ids=true, to_apply=%add | all-reduce | flops 32 | bytes 256
  17.9 11.7 %all-gather = s32[8,1,32]{2,1,0:T(1,128)} all-gather(s32[1,1,32]{2,1,0:T(1,128)S(1)} %bitcast.10), channel_id=1, replica_groups=mesh['row'=16,'col'=8] {'col'}, dimensions={0}, use_global_device_ids=true | all-gather | bytes 1152 | tf_op jit(solution)/shard_map/all_gather | solution.py:323
  29.7 67.8 %gather.1 = (bf16[2048,2048]{1,0:T(8,128)(2,1)}, bf16[512,2048]{1,0:T(8,128)(2,1)}, bf16[1024,2048]{1,0:T(8,128)(2,1)}) custom-call(bf16[2048,256]{1,0:T(8,128)(2,1)} %win.1, bf16[256,256]{1,0:T(8,128)(2,1)} %bitcast.8, bf16[512,256]{1,0:T(8,128)(2,1)} %pan.1), custom_call_target="tpu_custom_call" | custom-call | tf_op jit(solution)/shard_map/gather/pallas_call | solution.py:221
  97.5 37.9 %factor.1 = (bf16[512,256]{1,0:T(8,128)(2,1)}, bf16[2048,256]{1,0:T(8,128)(2,1)}, f32[512,1024]{1,0:T(8,128)}) custom-call(s32[8,32]{1,0:T(8,128)} %bitcast.9, s32[2]{0:T(128)} %pad_add_fusion.at, bf16[2048,2048]{1,0:T(8,128)(2,1)} %get-tuple-element.6.wg, bf16[512,2048]{1,0:T(8,128)(2,1)} %get-tuple-element.7.arow, ...), custom_call_target="tpu_custom_call" | custom-call | tf_op jit(solution)/shard_map/factor/pallas_call | solution.py:302
  (1 shorter events, 0.0 us)

commit v2 on v0

v2 whole, which is shorter than its diff:
```python
import jax
import jax.numpy as jnp
from jax import lax
from jax.experimental import pallas as pl
from jax.experimental.pallas import tpu as pltpu
from jax.sharding import PartitionSpec as P

B = 256
S = 16
H = 128
N = 8
BF = jnp.bfloat16
F32 = jnp.float32
MESH = pl.DeviceIdType.MESH


def place():
    row = lax.axis_index("row")
    col = lax.axis_index("col")
    return row, col, col // 2, row % 4, row // 4, col % 2


def bits_of(y, z):
    return [((y + 1) // 2) % 2, ((z + 1) // 2) % 2, y // 2, z // 2]


def address(bits, k):
    return sum(bits[(k + i) % 4] * 2**i for i in range(4))


def partners(y, z):
    ya = y + 1 - 2 * (y % 2)
    za = z + 1 - 2 * (z % 2)
    return [z * 4 + ya, za * 4 + y, z * 4 + 3 - y, (3 - z) * 4 + y]


def pick(a, b, c):
    return a * (1 - c) + b * c


def lanes(c):
    return pl.ds(pl.multiple_of(c * B, B), B)


def rows(start, count):
    return pl.ds(pl.multiple_of(start, S), count)


def lane(p):
    return slice(p * B, p * B + B)


def nt(a, b):
    return lax.dot_general(a, b, (((1,), (1,)), ((), ())), preferred_element_type=F32)


def kernel(
    live, win, inv, pan, trail, pan_out, win_out, trail_out,
    pv, kp, krow, kcol, wg, wf, u, ar, fr, am, fm, ao, tr, wo, po,
    wx_recv, wx_send, wh_recv, wh_send, wd_recv, wd_send,
    as_recv, as_send, ah_recv, ah_send, a3_recv, a3_send,
    ar_recv, ar_send, kr_recv, kr_send, kc_recv, kc_send, lsem, osem,
):
    row, col, x, y, z, core = place()
    bits = bits_of(y, z)
    addr = [address(bits, k) for k in range(4)]
    near = partners(y, z)
    other = 1 - core
    h = y % 2
    tcol = 2 * z + y // 2
    own = (z == x) & (y // 2 == core)

    def local(src, dst, sem):
        return pltpu.make_async_copy(src, dst, sem)

    def take(ref, sem):
        pltpu.make_async_copy(ref, ref, sem).wait()

    def remote(src, dst, ssem, rsem, r, c):
        return pltpu.make_async_remote_copy(
            src_ref=src, dst_ref=dst, send_sem=ssem, recv_sem=rsem, device_id=(r, c), device_id_type=MESH
        )

    load = local(pan, pv, lsem.at[0])
    load.start()
    load_trail = local(trail, tr, lsem.at[1])
    load_trail.start()

    barrier = pltpu.get_barrier_semaphore()

    def greet(r, c):
        pl.semaphore_signal(barrier, inc=1, device_id=(r, c), device_id_type=MESH)

    for d in range(1, 8):
        greet(row, (col + d) % 8)
    for k in range(4):
        greet(near[k], col)

    def greet_sources(t, carry):
        r, c = 2 * col + t // 8, t % 8

        @pl.when(jnp.logical_not((r == row) & (c == col)))
        def _():
            greet(r, c)

        return carry

    lax.fori_loop(0, 16, greet_sources, 0)

    l0 = live[0, 0]
    l1 = live[0, 1]
    load.wait()
    pv[B : 2 * B, :] = jnp.where(l0 == 1, pv[0:B, :], pv[B : 2 * B, :])
    keep0 = jnp.where(l0 == 0, 1.0, 0.0)
    keep1 = jnp.where((l0 == 1) | (l1 == 1), 1.0, 0.0)
    kp[...] = jnp.where(lax.broadcasted_iota(jnp.int32, (S, H), 0) == 0, keep0, keep1).astype(BF)

    pl.semaphore_wait(barrier, 27 - own.astype(jnp.int32))

    for j in range(4):

        @pl.when(x <= j)
        def _():
            for kc in range(2):
                q = 2 * j + kc
                t = addr[j] if kc == 0 else addr[3 - j]
                dst = wg.at[rows(q * B + t * S, S), lanes(col)]

                def send(src):
                    for d in range(4):
                        target = (x + d) % 4 * 2 + kc
                        if d == 0:

                            @pl.when(core == kc)
                            def _():
                                local(src, dst, wx_recv.at[j]).start()

                            @pl.when(core != kc)
                            def _():
                                remote(src, dst, wx_send.at[j], wx_recv.at[j], row, target).start()
                        else:
                            remote(src, dst, wx_send.at[j], wx_recv.at[j], row, target).start()

                @pl.when(q == col)
                def _():
                    send(inv.at[rows(t * S, S), :])

                @pl.when(q != col)
                def _():
                    send(win.at[rows(q * B + t * S, S), :])

    def scatter(t, carry):
        tbits = bits_of(t % 4, t // 4)
        mine = own & (t == row)
        kept = kcol.at[rows(h * S, S), pl.ds(pl.multiple_of(col * H, H), H)]

        @pl.when(mine)
        def _():
            local(kp, kept, kc_recv.at[h]).start()

        @pl.when(jnp.logical_not(mine))
        def _():
            remote(kp, kept, kc_send, kc_recv.at[h], t, tcol).start()

        for kk in range(2):
            s = pick(address(tbits, kk), address(tbits, 2 + kk), h)
            src = pv.at[rows(kk * B + s * S, S), :]
            k = 2 * h + kk
            dst = am.at[rows(k * H + s % 8 * S, S), lanes(col)]

            @pl.when(mine)
            def _():
                local(src, dst, as_recv.at[k]).start()

            @pl.when(jnp.logical_not(mine))
            def _():
                remote(src, dst, as_send, as_recv.at[k], t, tcol).start()

        return carry

    def w_base(j, i):
        n = 2**i
        return pick(addr[j], addr[3 - j], core) // n * n

    def w_part(j, base, n, c):
        return wg.at[rows((2 * j + c) * B + base * S, n * S), pl.ds(0, B * (2 * j + 2))]

    def w_got(j, i):
        n = 2**i
        a = pick(addr[j], addr[3 - j], core)
        return w_part(j, a // (2 * n) * (2 * n) + (1 - a // n % 2) * n, n, core)

    def w_step(i):
        for j in range(4):
            if i == 0:
                take(w_part(j, w_base(j, 0), 1, core), wx_recv.at[j])
            else:
                take(w_got(j, i - 1), wh_recv.at[i - 1, j])
            part = w_part(j, w_base(j, i), 2**i, core)
            to = pick(near[(j + i) % 4], near[(3 - j + i) % 4], core)
            remote(part, part, wh_send.at[i, j], wh_recv.at[i, j], to, col).start()
            if i == 3:
                remote(part, part, wd_send.at[j, 0], wd_recv.at[j, 0], row, x * 2 + other).start()

    def a_part(k, base, n):
        return am.at[rows(k * H + base * S, n * S), :]

    def a_got(k, i):
        n = 2**i
        a = addr[k] % 8
        return a_part(k, a // (2 * n) * (2 * n) + (1 - a // n % 2) * n, n)

    def a_step(i):
        n = 2**i
        for k in range(4):
            if i == 0:
                take(a_part(k, addr[k] % 8, 1), as_recv.at[k])
            else:
                take(a_got(k, i - 1), ah_recv.at[i - 1, k])
            if i < 3:
                part = a_part(k, addr[k] % 8 // n * n, n)
                remote(part, part, ah_send.at[i, k], ah_recv.at[i, k], near[(k + i) % 4], col).start()
        if i == 3:
            for g in range(4):
                for k in range(4):
                    there = slice(k * H, k * H + H), slice(g * 2 * B, g * 2 * B + 2 * B)
                    remote(
                        am.at[there], ao.at[there], a3_send.at[g, k], a3_recv.at[g, k], near[(k + 3) % 4], col
                    ).start()

    lax.fori_loop(0, 16, scatter, 0)
    w_step(0)

    mine = ar.at[:, lanes(col)]
    kept = krow.at[:, pl.ds(pl.multiple_of(col * H, H), H)]
    local(pv, mine, lsem.at[2]).start()
    local(kp, kept, kr_recv).start()
    for d in range(1, 8):
        remote(kp, kept, kr_send, kr_recv, row, (col + d) % 8).start()
    for d in range(1, 4):
        remote(pv, mine, ar_send.at[d - 1], ar_recv.at[col], row, (x + d) % 4 * 2 + core).start()
    remote(pv, mine, ar_send.at[3], ar_recv.at[col], row, x * 2 + other).start()

    w_step(1)
    a_step(0)
    w_step(2)
    a_step(1)
    w_step(3)
    a_step(2)

    for d in range(1, 4):
        c = (x + 4 - d) % 4 * 2 + core
        got = ar.at[:, lanes(c)]
        take(got, ar_recv.at[c])
        remote(got, got, ar_send.at[3 + d], ar_recv.at[c], row, x * 2 + other).start()
    for j in range(4):
        got = w_got(j, 3)
        take(got, wh_recv.at[3, j])
        remote(got, got, wd_send.at[j, 1], wd_recv.at[j, 1], row, x * 2 + other).start()
    a_step(3)
    for d in range(4):
        c = (x + d) % 4 * 2 + other
        take(ar.at[:, lanes(c)], ar_recv.at[c])
    local(pv, mine, lsem.at[2]).wait()
    take(krow, kr_recv)
    for j in range(4):
        a = pick(addr[3 - j], addr[j], core) // 8
        take(w_part(j, a * 8, 8, other), wd_recv.at[j, 0])
        take(w_part(j, (1 - a) * 8, 8, other), wd_recv.at[j, 1])

    def keep(ref, first, i, p):
        t = ref[first : first + S, p * H : p * H + H].astype(F32)[i : i + 1, :]
        return jnp.concatenate([t, t], axis=1) > 0.5

    def masked(value, mask):
        return jnp.where(mask, value, 0.0).astype(BF)

    for p in range(N):
        diag = wg[lane(p), lane(p)]
        if p > 0:
            prev = jnp.dot(diag, wf[lane(p), : p * B], preferred_element_type=F32)
            u[lane(p), : p * B] = (-prev).astype(BF)
        u[lane(p), lane(p)] = diag
        up = u[lane(p), : (p + 1) * B]

        def operand(factors, raw, at):
            if p == 0:
                return raw[at, lane(p)]
            return jnp.concatenate([factors[at, : p * B], raw[at, lane(p)]], axis=1)

        for q in range(p + 1, N):
            wf[lane(q), lane(p)] = nt(operand(wf, wg, lane(q)), up).astype(BF)
        for i in range(2):
            fr[lane(i), lane(p)] = masked(nt(operand(fr, ar, lane(i)), up), keep(krow, 0, i, p))

    here = lanes(col)
    for q in range(N):
        block = wf[lane(q), here]
        wo[lane(q), :] = jnp.where(q > col, block, jnp.zeros_like(block))
    local(wo, win_out, osem.at[0]).start()
    f0 = fr[0:B, here]
    f1 = fr[B : 2 * B, here]
    po[0:B, :] = jnp.where(l0 == 0, f0, f1)
    po[B : 2 * B, :] = jnp.where(l0 == 0, f1, jnp.zeros_like(f1))
    local(po, pan_out, osem.at[1]).start()

    take(kcol.at[0:S, :], kc_recv.at[0])
    take(kcol.at[S : 2 * S, :], kc_recv.at[1])

    def solve(p, factors, raw):
        up = u[lane(p), : (p + 1) * B]
        z_in = raw[:, lane(p)]
        if p > 0:
            z_in = jnp.concatenate([factors[:, : p * B], z_in], axis=1)
        out = nt(z_in, up)
        for k in range(4):
            part = slice(k * H, k * H + H)
            factors[part, lane(p)] = masked(out[part, :], keep(kcol, k // 2 * S, k % 2, p))

    load_trail.wait()

    def update(factors, far):
        for g in range(2):
            prod = nt(fr[...], factors[lane(g), :])
            for e in range(2):
                k = 2 * g + e
                half = addr[k] // 8
                if far:
                    half = 1 - half
                at = pl.ds(pl.multiple_of(k * B + half * H, H), H)
                tr[:, at] = tr[:, at] - prod[:, e * H : e * H + H]
                local(tr.at[:, at], trail_out.at[:, at], osem.at[2 + 4 * far + k]).start()

    for p in range(N):
        solve(p, fm, am)
    update(fm, 0)
    for p in range(N):
        if p % 2 == 0:
            for k in range(4):
                g = p // 2
                take(ao.at[k * H : k * H + H, g * 2 * B : g * 2 * B + 2 * B], a3_recv.at[g, k])
        solve(p, ao, ao)
    update(ao, 1)

    for j in range(4):

        @pl.when(x <= j)
        def _():
            take(pv.at[pl.ds(0, 7 * S), :], wx_send.at[j])

        for i in range(4):
            take(w_part(j, w_base(j, i), 2**i, core), wh_send.at[i, j])
        take(w_part(j, w_base(j, 3), 8, core), wd_send.at[j, 0])
        take(w_got(j, 3), wd_send.at[j, 1])
        for i in range(3):
            n = 2**i
            take(a_part(j, addr[j] % 8 // n * n, n), ah_send.at[i, j])
        for g in range(4):
            take(am.at[j * H : j * H + H, g * 2 * B : g * 2 * B + 2 * B], a3_send.at[g, j])
    for d in range(7):
        take(pv, ar_send.at[d])
    take(krow.at[:, 0 : 7 * H], kr_send)

    @pl.when(own)
    def _():
        take(pv.at[pl.ds(0, 30 * S), :], as_send)
        take(am.at[0:S, 0 : 15 * H], kc_send)

    @pl.when(jnp.logical_not(own))
    def _():
        take(pv, as_send)
        take(am.at[0:S, 0 : 16 * H], kc_send)

    local(wo, win_out, osem.at[0]).wait()
    local(po, pan_out, osem.at[1]).wait()
    for far in range(2):
        for k in range(4):
            half = addr[k] // 8
            if far:
                half = 1 - half
            at = pl.ds(pl.multiple_of(k * B + half * H, H), H)
            local(tr.at[:, at], trail_out.at[:, at], osem.at[2 + 4 * far + k]).wait()


def fused(live, win, inv, pan, trail):
    dma = pltpu.SemaphoreType.DMA
    anys = pl.BlockSpec(memory_space=pl.ANY)
    smem = pl.BlockSpec(memory_space=pltpu.SMEM)
    vmem = pltpu.VMEM
    return pl.pallas_call(
        kernel,
        out_shape=(
            jax.ShapeDtypeStruct((2 * B, B), BF),
            jax.ShapeDtypeStruct((N * B, B), BF),
            jax.ShapeDtypeStruct((2 * B, 4 * B), F32),
        ),
        in_specs=[smem] + [anys] * 4,
        out_specs=(anys,) * 3,
        scratch_shapes=[
            vmem((2 * B, B), BF),
            vmem((S, H), BF),
            vmem((S, N * H), BF),
            vmem((2 * S, N * H), BF),
            vmem((N * B, N * B), BF),
            vmem((N * B, N * B), BF),
            vmem((N * B, N * B), BF),
            vmem((2 * B, N * B), BF),
            vmem((2 * B, N * B), BF),
            vmem((2 * B, N * B), BF),
            vmem((2 * B, N * B), BF),
            vmem((2 * B, N * B), BF),
            vmem((2 * B, 4 * B), F32),
            vmem((N * B, B), BF),
            vmem((2 * B, B), BF),
            dma((4,)), dma((4,)), dma((4, 4)), dma((4, 4)), dma((4, 2)), dma((4, 2)),
            dma((4,)), dma(()), dma((3, 4)), dma((3, 4)), dma((4, 4)), dma((4, 4)),
            dma((8,)), dma((7,)), dma(()), dma(()), dma((2,)), dma(()), dma((3,)), dma((10,)),
        ],
        compiler_params=pltpu.CompilerParams(
            has_side_effects=True, collective_id=0, vmem_limit_bytes=58 * 2**20
        ),
        name="fused",
    )(live, win, inv, pan, trail)


def local_part(panel_blocks, live_rows, window_blocks, diag_inverse, trailing):
    return fused(live_rows, window_blocks, diag_inverse[0], panel_blocks, trailing)


def solution(mesh):
    return jax.shard_map(
        local_part,
        mesh=mesh,
        in_specs=(
            P("row", "col"),
            P("col", "row"),
            P(None, "col"),
            P("col", None, None),
            P("row", "col"),
        ),
        out_specs=(P("row", "col"), P(None, "col"), P("row", "col")),
        check_vma=False,
    )
```

time: 699 us -> 83.3 us (0.12)
  waiting for transfers between devices: 588 us -> 0 us
  Pallas kernels: 0 us -> 75.8 us
  matrix products: 44.4 us -> 0 us
  other arithmetic: 25.3 us -> 0 us
  local copies, waits for them, and re-layouts: 25.1 us -> 5.4 us
  between operations: 14.6 us -> 0.65 us
    psum x9 -> x0, waiting for transfers between devices: 588 us -> none  [broadcast(): return lax.psum(jnp.where(mine, value, jnp.zeros_like(value)), axis)]
    pallas_call x0 -> x1, Pallas kernels: none -> 75.8 us  [fused(): pl.pallas_call(kernel, out_shape=(jax.ShapeDtypeStruct((2 * B, B), BF), j...]
    dot_general x39 -> x0, matrix products: 44.4 us -> none  [the longest x7 11.5 us: local(): jnp.dot(window_here, w_block.T, preferred_element_type=jnp.float32)]
    select_n x16 -> x0, other arithmetic: 16.4 us -> none  [the longest x15 16.4 us: broadcast(): return lax.psum(jnp.where(mine, value, jnp.zeros_like(value)), axis)]
    another operation x15 -> x0, local copies, waits for them, and re-layouts: 10.4 us -> none
  transfers between devices with their start and end apart: 9 -> 0, of which waited for: 9 -> 0; matrix products, arithmetic and copies ran while one was open for 2% -> 0% of each run, Pallas kernels for 0% -> 0%
where the time goes in v2:
time: 83.3 us; the launch traced here: 81.9 us
  Pallas kernels  75.8 us (91%)
  local copies, waits for them, and re-layouts  5.4 us (6%)
    pallas_call x1, Pallas kernels, fused(): pl.pallas_call(kernel, out_shape=(jax.ShapeDtypeStruct((2 * B, B), BF), j...  75.8 us
    unnamed x5, local copies, waits for them, and re-layouts  5.4 us

profile of v2, /device:TPU:1, one launch (start us, length us, event | category | flops | bytes accessed | tf_op | source)
XLA Modules:
  0.0 81.9 jit_solution(4345826296407719430)
XLA Ops:
  0.6 75.8 %fused.1 = (bf16[512,256]{1,0:T(8,128)(2,1)}, bf16[2048,256]{1,0:T(8,128)(2,1)}, f32[512,1024]{1,0:T(8,128)}) custom-call(s32[1,2]{1,0:T(1,128)} %live.1, bf16[2048,256]{1,0:T(8,128)(2,1)} %win.1, bf16[256,256]{1,0:T(8,128)(2,1)} %bitcast.1, bf16[512,256]{1,0:T(8,128)(2,1)} %pan.1, f32[512,1024]{1,0:T(8,128)} %trail.1), custom_call_target="tpu_custom_call" | custom-call | tf_op jit(solution)/shard_map/fused/pallas_call | solution.py:390
  76.5 0.0 copy-start
  76.5 1.8 %copy.11 = bf16[512,256]{1,0:T(8,128)(2,1)} copy(bf16[512,256]{1,0:T(8,128)(2,1)} %get-tuple-element.6) | data formatting | bytes 524288
  78.3 2.3 %copy.12 = bf16[2048,256]{1,0:T(8,128)(2,1)} copy(bf16[2048,256]{1,0:T(8,128)(2,1)} %get-tuple-element.7) | data formatting | bytes 2097152
  80.6 0.0 copy-done
  80.6 1.3 %copy.13 = f32[512,1024]{1,0:T(8,128)} copy(f32[512,1024]{1,0:T(8,128)S(1)} %copy-done) | data formatting | bytes 4194304
Async XLA Ops:
  76.5 4.1 %copy-start = (f32[512,1024]{1,0:T(8,128)S(1)}, f32[512,1024]{1,0:T(8,128)}, u32[]{:S(2)}) copy-start(f32[512,1024]{1,0:T(8,128)} %get-tuple-element.8) | copy-start | bytes 6291460

commit v3 on v2

v3 whole, which is shorter than its diff:
```python
import jax
import jax.numpy as jnp
from jax import lax
from jax.experimental import pallas as pl
from jax.experimental.pallas import tpu as pltpu
from jax.sharding import PartitionSpec as P

B = 256
S = 16
H = 128
N = 8
BF = jnp.bfloat16
F32 = jnp.float32
MESH = pl.DeviceIdType.MESH


def place():
    row = lax.axis_index("row")
    col = lax.axis_index("col")
    return row, col, col // 2, row % 4, row // 4, col % 2


def bits_of(y, z):
    return [((y + 1) // 2) % 2, ((z + 1) // 2) % 2, y // 2, z // 2]


def address(bits, k):
    return sum(bits[(k + i) % 4] * 2**i for i in range(4))


def partners(y, z):
    ya = y + 1 - 2 * (y % 2)
    za = z + 1 - 2 * (z % 2)
    return [z * 4 + ya, za * 4 + y, z * 4 + 3 - y, (3 - z) * 4 + y]


def pick(a, b, c):
    return a * (1 - c) + b * c


def lanes(c):
    return pl.ds(pl.multiple_of(c * B, B), B)


def rows(start, count):
    return pl.ds(pl.multiple_of(start, S), count)


def lane(p):
    return slice(p * B, p * B + B)


def nt(a, b):
    return lax.dot_general(a, b, (((1,), (1,)), ((), ())), preferred_element_type=F32)


def kernel(
    live, win, inv, pan, trail, pan_out, win_out, trail_out,
    pv, pp, st, a0, kp, krow, kcol, iv, wc, wg, wf, u, ar, fr, am, fm, ao, tr, wo, po,
    wx_recv, wx_send, wh_recv, wh_send, wd_recv, wd_send, wr_recv, wr_send, we_recv, we_send,
    a1_recv, a1_send, a2_recv, a2_send, ah_recv, ah_send, a3_recv, a3_send,
    ar_recv, ar_send, ad_recv, ad_send, kr_recv, kr_send, kc_recv, kc_send, lsem, osem,
):
    row, col, x, y, z, core = place()
    bits = bits_of(y, z)
    addr = [address(bits, k) for k in range(4)]
    near = partners(y, z)
    other = 1 - core
    h = y % 2
    sibling = x * 2 + other
    own = (z == x) & (y // 2 == core)

    def local(src, dst, sem):
        return pltpu.make_async_copy(src, dst, sem)

    def take(ref, sem):
        pltpu.make_async_copy(ref, ref, sem).wait()

    def remote(src, dst, ssem, rsem, r, c):
        return pltpu.make_async_remote_copy(
            src_ref=src, dst_ref=dst, send_sem=ssem, recv_sem=rsem, device_id=(r, c), device_id_type=MESH
        )

    load = local(pan, pv, lsem.at[0])
    load.start()
    load_window = local(win, wc, lsem.at[1])
    load_window.start()
    load_inverse = local(inv, iv, lsem.at[3])
    load_inverse.start()
    load_trail = local(trail, tr, lsem.at[2])
    load_trail.start()

    barrier = pltpu.get_barrier_semaphore()

    def greet(r, c):
        pl.semaphore_signal(barrier, inc=1, device_id=(r, c), device_id_type=MESH)

    for d in range(1, 8):
        greet(row, (col + d) % 8)
    for d in range(1, 16):
        greet((row + d) % 16, col)

    l0 = live[0, 0]
    l1 = live[0, 1]
    load.wait()
    pv[B : 2 * B, :] = jnp.where(l0 == 1, pv[0:B, :], pv[B : 2 * B, :])
    keep0 = jnp.where(l0 == 0, 1.0, 0.0)
    keep1 = jnp.where((l0 == 1) | (l1 == 1), 1.0, 0.0)
    kp[...] = jnp.where(lax.broadcasted_iota(jnp.int32, (S, H), 0) == 0, keep0, keep1).astype(BF)
    for t in range(16):
        tbits = bits_of(t % 4, t // 4)
        for kk in range(2):
            s = pick(address(tbits, kk), address(tbits, 2 + kk), h)
            pp[t * 2 * S + kk * S : t * 2 * S + kk * S + S, :] = pv[rows(kk * B + s * S, S), :]

    pl.semaphore_wait(barrier, 22)

    mine = st.at[rows(row * 2 * S, 2 * S), :]
    local(pp.at[rows(row * 2 * S, 2 * S), :], mine, a1_recv).start()

    def scatter(d, carry):
        t = (row + d) % 16
        remote(pp.at[rows(t * 2 * S, 2 * S), :], mine, a1_send, a1_recv, t, col).start()
        return carry

    lax.fori_loop(1, 16, scatter, 0)

    load_window.wait()
    load_inverse.wait()
    wc[lanes(col), :] = iv[...]
    for j in range(4):

        @pl.when(x <= (0, 1, 0, 2)[j])
        def _():
            for kc in range(2):
                t = addr[j] if kc == 0 else addr[3 - j]
                at = rows((2 * j + kc) * B + t * S, S)
                src = wc.at[at, :]
                dst = wg.at[at, lanes(col)]
                for d in range(4):
                    target = (x + d) % 4 * 2 + kc
                    if d == 0:

                        @pl.when(core == kc)
                        def _():
                            local(src, dst, wx_recv.at[j]).start()

                        @pl.when(core != kc)
                        def _():
                            remote(src, dst, wx_send.at[j], wx_recv.at[j], row, target).start()
                    else:
                        remote(src, dst, wx_send.at[j], wx_recv.at[j], row, target).start()

    def w_width(j):
        return (2, 4, 2, 6)[j] * B

    def w_base(j, i):
        n = 2**i
        return pick(addr[j], addr[3 - j], core) // n * n

    def w_part(j, base, n, c):
        return wg.at[rows((2 * j + c) * B + base * S, n * S), pl.ds(0, w_width(j))]

    def w_got(j, i):
        n = 2**i
        a = pick(addr[j], addr[3 - j], core)
        return w_part(j, a // (2 * n) * (2 * n) + (1 - a // n % 2) * n, n, core)

    def w_step(i):
        for j in range(4):
            if i == 0:
                take(w_part(j, w_base(j, 0), 1, core), wx_recv.at[j])
            else:
                take(w_got(j, i - 1), wh_recv.at[i - 1, j])
            part = w_part(j, w_base(j, i), 2**i, core)
            to = pick(near[(j + i) % 4], near[(3 - j + i) % 4], core)
            remote(part, part, wh_send.at[i, j], wh_recv.at[i, j], to, col).start()
            if i == 3:
                remote(part, part, wd_send.at[j, 0], wd_recv.at[j, 0], row, sibling).start()

    def a_part(k, base, n, g):
        return am.at[rows(k * H + base * S, n * S), slice(g * 4 * B, g * 4 * B + 4 * B)]

    def a_got(k, i, g):
        n = 2**i
        a = addr[k] % 8
        return a_part(k, a // (2 * n) * (2 * n) + (1 - a // n % 2) * n, n, g)

    def a_step(i, g):
        n = 2**i
        chunk = slice(g * 4 * B, g * 4 * B + 4 * B)
        if i == 0:
            take(a0.at[:, chunk], a2_recv.at[g])
            for k in range(4):
                am[rows(k * H + addr[k] % 8 * S, S), chunk] = a0[k * S : k * S + S, chunk]
        for k in range(4):
            if i > 0:
                take(a_got(k, i - 1, g), ah_recv.at[i - 1, g, k])
            if i < 3:
                part = a_part(k, addr[k] % 8 // n * n, n, g)
                remote(part, part, ah_send.at[i, g, k], ah_recv.at[i, g, k], near[(k + i) % 4], col).start()
        if i == 3:
            for g2 in (2 * g, 2 * g + 1):
                for k in range(4):
                    there = slice(k * H, k * H + H), slice(g2 * 2 * B, g2 * 2 * B + 2 * B)
                    remote(
                        am.at[there], ao.at[there], a3_send.at[g2, k], a3_recv.at[g2, k], near[(k + 3) % 4], col
                    ).start()

    pieces = [(1, 0), (2, 0), (3, 1)]

    def piece(n, c):
        xs, hf = pieces[n]
        return (4 + 2 * hf) * B, lanes(2 * xs + c)

    def whole_send(n):
        xs, hf = pieces[n]

        @pl.when(x == xs)
        def _():
            first, at = piece(n, core)
            src = wc.at[first : first + 2 * B, :]
            dst = wg.at[first : first + 2 * B, at]
            local(src, dst, wr_recv.at[n]).start()
            for d in range(1, 4):
                remote(src, dst, wr_send.at[n, d - 1], wr_recv.at[n], row, (x + d) % 4 * 2 + core).start()

    def whole_share(n):
        xs, hf = pieces[n]
        first, at = piece(n, core)
        got = wg.at[first : first + 2 * B, at]
        take(got, wr_recv.at[n])
        remote(got, got, we_send.at[n], we_recv.at[n], row, sibling).start()

    def whole_take(n):
        first, at = piece(n, other)
        take(wg.at[first : first + 2 * B, at], we_recv.at[n])

    w_step(0)
    take(st, a1_recv)
    for d in range(4):
        xd = (x + d) % 4
        for kc in range(2):
            src = st.at[rows((4 * xd + 2 * kc) * 2 * S, 4 * S), :]
            dst = a0.at[:, lanes(col)]
            if d == 0:

                @pl.when(core == kc)
                def _():
                    local(src, dst, a2_recv.at[x // 2]).start()

                @pl.when(core != kc)
                def _():
                    remote(src, dst, a2_send, a2_recv.at[x // 2], row, sibling).start()
            else:
                remote(src, dst, a2_send, a2_recv.at[x // 2], row, xd * 2 + kc).start()

    w_step(1)
    kept = krow.at[:, pl.ds(pl.multiple_of(col * H, H), H)]
    local(kp, kept, kr_recv).start()
    for d in range(1, 8):
        remote(kp, kept, kr_send, kr_recv, row, (col + d) % 8).start()
    for n in range(len(pieces)):
        whole_send(n)
    w_step(2)
    a_step(0, 0)
    a_step(0, 1)
    w_step(3)

    panel = ar.at[:, lanes(col)]
    local(pv, panel, lsem.at[0]).start()
    for d in range(1, 4):
        remote(pv, panel, ar_send.at[d - 1], ar_recv.at[d - 1], row, (x + d) % 4 * 2 + core).start()
    remote(pv, panel, ad_send.at[0], ad_recv.at[0], row, sibling).start()

    a_step(1, 0)
    a_step(1, 1)

    take(krow, kr_recv)

    @pl.when(own)
    def _():
        dst = kcol.at[rows(h * S, S), :]
        local(krow, dst, kc_recv.at[h]).start()
        for d in range(1, 16):
            remote(krow, dst, kc_send, kc_recv.at[h], (row + d) % 16, col).start()

    for j in range(4):
        got = w_got(j, 3)
        take(got, wh_recv.at[3, j])
        remote(got, got, wd_send.at[j, 1], wd_recv.at[j, 1], row, sibling).start()
    a_step(2, 0)
    a_step(2, 1)
    for n in range(len(pieces)):
        whole_share(n)
    for j in range(4):
        a = pick(addr[3 - j], addr[j], core) // 8
        take(w_part(j, a * 8, 8, other), wd_recv.at[j, 0])
        take(w_part(j, (1 - a) * 8, 8, other), wd_recv.at[j, 1])

    def keep(ref, first, i, p):
        t = ref[first : first + S, p * H : p * H + H].astype(F32)[i : i + 1, :]
        return jnp.concatenate([t, t], axis=1) > 0.5

    def masked(value, mask):
        return jnp.where(mask, value, 0.0).astype(BF)

    def operand(factors, raw, at, p):
        if p == 0:
            return raw[at, lane(p)]
        return jnp.concatenate([factors[at, : p * B], raw[at, lane(p)]], axis=1)

    for p in range(N):
        if p == 2:
            whole_take(0)
        if p == 4:
            a_step(3, 0)
        if p == 6:
            a_step(3, 1)
        if p == 4:
            whole_take(1)
        if p == 6:
            whole_take(2)
        diag = wg[lane(p), lane(p)]
        if p > 0:
            prev = jnp.dot(diag, wf[lane(p), : p * B], preferred_element_type=F32)
            u[lane(p), : p * B] = (-prev).astype(BF)
        u[lane(p), lane(p)] = diag
        up = u[lane(p), : (p + 1) * B]
        for q in range(p + 1, N):
            wf[lane(q), lane(p)] = nt(operand(wf, wg, lane(q), p), up).astype(BF)

    here = lanes(col)
    for q in range(N):
        block = wf[lane(q), here]
        wo[lane(q), :] = jnp.where(q > col, block, jnp.zeros_like(block))
    local(wo, win_out, osem.at[0]).start()

    take(kcol.at[0:S, :], kc_recv.at[0])
    take(kcol.at[S : 2 * S, :], kc_recv.at[1])

    def solve(p, factors, raw):
        up = u[lane(p), : (p + 1) * B]
        out = nt(operand(factors, raw, slice(0, 2 * B), p), up)
        for k in range(4):
            part = slice(k * H, k * H + H)
            factors[part, lane(p)] = masked(out[part, :], keep(kcol, k // 2 * S, k % 2, p))

    def update(factors, far, first, last):
        for g in range(2):
            prod = nt(fr[:, first:last], factors[lane(g), first:last])
            for e in range(2):
                k = 2 * g + e
                half = addr[k] // 8
                if far:
                    half = 1 - half
                at = pl.ds(pl.multiple_of(k * B + half * H, H), H)
                tr[:, at] = tr[:, at] - prod[:, e * H : e * H + H]
                if last == N * B:
                    local(tr.at[:, at], trail_out.at[:, at], osem.at[2 + 4 * far + k]).start()

    def solve_far(p):
        if p % 2 == 0:
            for k in range(4):
                g = p // 2
                take(ao.at[k * H : k * H + H, g * 2 * B : g * 2 * B + 2 * B], a3_recv.at[g, k])
        solve(p, ao, ao)

    for d in range(1, 4):
        got = ar.at[:, lanes((x + 4 - d) % 4 * 2 + core)]
        take(got, ar_recv.at[d - 1])
        remote(got, got, ad_send.at[d], ad_recv.at[d], row, sibling).start()
    local(pv, panel, lsem.at[0]).wait()
    for d in range(4):
        take(ar.at[:, lanes((x + 4 - d) % 4 * 2 + other)], ad_recv.at[d])
    for p in range(N):
        solve(p, fm, am)
    for p in range(N):
        up = u[lane(p), : (p + 1) * B]
        for i in range(2):
            fr[lane(i), lane(p)] = masked(nt(operand(fr, ar, lane(i), p), up), keep(krow, 0, i, p))
    f0 = fr[0:B, here]
    f1 = fr[B : 2 * B, here]
    po[0:B, :] = jnp.where(l0 == 0, f0, f1)
    po[B : 2 * B, :] = jnp.where(l0 == 0, f1, jnp.zeros_like(f1))
    local(po, pan_out, osem.at[1]).start()

    load_trail.wait()
    update(fm, 0, 0, N * B)
    for p in range(4):
        solve_far(p)

    solve_far(4)
    solve_far(5)
    update(ao, 1, 0, 6 * B)
    solve_far(6)
    solve_far(7)
    update(ao, 1, 6 * B, N * B)

    for j in range(4):

        @pl.when(x <= (0, 1, 0, 2)[j])
        def _():
            take(pv.at[pl.ds(0, 7 * S), :], wx_send.at[j])

        for i in range(4):
            take(w_part(j, w_base(j, i), 2**i, core), wh_send.at[i, j])
        take(w_part(j, w_base(j, 3), 8, core), wd_send.at[j, 0])
        take(w_got(j, 3), wd_send.at[j, 1])
        for i in range(3):
            n = 2**i
            for g in range(2):
                take(a_part(j, addr[j] % 8 // n * n, n, g), ah_send.at[i, g, j])
        for g in range(4):
            take(am.at[j * H : j * H + H, g * 2 * B : g * 2 * B + 2 * B], a3_send.at[g, j])
    take(pv.at[pl.ds(0, 15 * 2 * S), :], a1_send)
    take(pv.at[pl.ds(0, 7 * 4 * S), :], a2_send)
    for n in range(len(pieces)):
        xs, hf = pieces[n]
        take(pv, we_send.at[n])

        @pl.when(x == xs)
        def _():
            for d in range(3):
                take(pv, wr_send.at[n, d])

    for d in range(4):
        take(pv, ad_send.at[d])
        if d < 3:
            take(pv, ar_send.at[d])
    take(krow.at[:, 0 : 7 * H], kr_send)

    @pl.when(own)
    def _():
        take(ar.at[0 : 15 * S, 0 : N * H], kc_send)

    local(wo, win_out, osem.at[0]).wait()
    local(po, pan_out, osem.at[1]).wait()
    for far in range(2):
        for k in range(4):
            half = addr[k] // 8
            if far:
                half = 1 - half
            at = pl.ds(pl.multiple_of(k * B + half * H, H), H)
            local(tr.at[:, at], trail_out.at[:, at], osem.at[2 + 4 * far + k]).wait()


def fused(live, win, inv, pan, trail):
    dma = pltpu.SemaphoreType.DMA
    anys = pl.BlockSpec(memory_space=pl.ANY)
    smem = pl.BlockSpec(memory_space=pltpu.SMEM)
    vmem = pltpu.VMEM
    return pl.pallas_call(
        kernel,
        out_shape=(
            jax.ShapeDtypeStruct((2 * B, B), BF),
            jax.ShapeDtypeStruct((N * B, B), BF),
            jax.ShapeDtypeStruct((2 * B, 4 * B), F32),
        ),
        in_specs=[smem] + [anys] * 4,
        out_specs=(anys,) * 3,
        scratch_shapes=[
            vmem((2 * B, B), BF),
            vmem((2 * B, B), BF),
            vmem((2 * B, B), BF),
            vmem((4 * S, N * B), BF),
            vmem((S, H), BF),
            vmem((S, N * H), BF),
            vmem((2 * S, N * H), BF),
            vmem((B, B), BF),
            vmem((N * B, B), BF),
            vmem((N * B, N * B), BF),
            vmem((N * B, N * B), BF),
            vmem((N * B, N * B), BF),
            vmem((2 * B, N * B), BF),
            vmem((2 * B, N * B), BF),
            vmem((2 * B, N * B), BF),
            vmem((2 * B, N * B), BF),
            vmem((2 * B, N * B), BF),
            vmem((2 * B, 4 * B), F32),
            vmem((N * B, B), BF),
            vmem((2 * B, B), BF),
            dma((4,)), dma((4,)), dma((4, 4)), dma((4, 4)), dma((4, 2)), dma((4, 2)),
            dma((3,)), dma((3, 3)), dma((3,)), dma((3,)),
            dma(()), dma(()), dma((2,)), dma(()), dma((3, 2, 4)), dma((3, 2, 4)), dma((4, 4)), dma((4, 4)),
            dma((3,)), dma((3,)), dma((4,)), dma((4,)), dma(()), dma(()), dma((2,)), dma(()),
            dma((4,)), dma((10,)),
        ],
        compiler_params=pltpu.CompilerParams(
            has_side_effects=True, collective_id=0, vmem_limit_bytes=58 * 2**20
        ),
        name="fused",
    )(live, win, inv, pan, trail)


def hand_out_kernel(pan, win, trail, pan_out, win_out, trail_out, pv, wv, tv, load, store):
    parts = [(pan, pv, pan_out, 0, 512)]
    parts += [(win, wv, win_out, i * 1024, 1024) for i in range(2)]
    parts += [(trail, tv, trail_out, i * 128, 128) for i in range(4)]

    def move(n, inward):
        src, mid, dst, first, count = parts[n]
        at = slice(first, first + count)
        if inward:
            return pltpu.make_async_copy(src.at[at, :], mid.at[at, :], load.at[n])
        return pltpu.make_async_copy(mid.at[at, :], dst.at[at, :], store.at[n])

    for n in range(len(parts)):
        move(n, True).start()
    for n in range(len(parts)):
        move(n, True).wait()
        move(n, False).start()
    for n in range(len(parts)):
        move(n, False).wait()


def hand_out(*arrays):
    anys = pl.BlockSpec(memory_space=pl.ANY)
    dma = pltpu.SemaphoreType.DMA
    return pl.pallas_call(
        hand_out_kernel,
        out_shape=tuple(jax.ShapeDtypeStruct(a.shape, a.dtype) for a in arrays),
        in_specs=[anys] * 3,
        out_specs=(anys,) * 3,
        scratch_shapes=[pltpu.VMEM(a.shape, a.dtype) for a in arrays] + [dma((7,)), dma((7,))],
        name="hand_out",
    )(*arrays)


def local_part(panel_blocks, live_rows, window_blocks, diag_inverse, trailing):
    return hand_out(*fused(live_rows, window_blocks, diag_inverse[0], panel_blocks, trailing))


def solution(mesh):
    return jax.shard_map(
        local_part,
        mesh=mesh,
        in_specs=(
            P("row", "col"),
            P("col", "row"),
            P(None, "col"),
            P("col", None, None),
            P("row", "col"),
        ),
        out_specs=(P("row", "col"), P(None, "col"), P("row", "col")),
        check_vma=False,
    )
```

time: 83.3 us -> 65.6 us (0.79); the launches traced: 81.9 us -> 65.1 us
  Pallas kernels: 75.8 us -> 64.5 us
  local copies, waits for them, and re-layouts: 5.4 us -> 0 us
    pallas_call x1, Pallas kernels: 75.8 us -> 61.6 us  [fused(): pl.pallas_call(kernel, out_shape=(jax.ShapeDtypeStruct((2 * B, B), BF), j...]
    unnamed x5 -> x0, local copies, waits for them, and re-layouts: 5.4 us -> none
    pallas_call x0 -> x1, Pallas kernels: none -> 2.92 us  [hand_out(): pl.pallas_call(hand_out_kernel, out_shape=tuple((jax.ShapeDtypeStruct(a.s...]
where the time goes in v3:
time: 65.6 us; the launch traced here: 65.1 us
  Pallas kernels  64.5 us (98%)
    pallas_call x1, Pallas kernels, fused(): pl.pallas_call(kernel, out_shape=(jax.ShapeDtypeStruct((2 * B, B), BF), j...  61.6 us
    pallas_call x1, Pallas kernels, hand_out(): pl.pallas_call(hand_out_kernel, out_shape=tuple((jax.ShapeDtypeStruct(a.s...  2.92 us

profile of v3, /device:TPU:1, one launch (start us, length us, event | category | flops | bytes accessed | tf_op | source)
XLA Modules:
  0.0 65.1 jit_solution(3175473416896041500)
XLA Ops:
  0.6 61.6 %fused.1 = (bf16[512,256]{1,0:T(8,128)(2,1)}, bf16[2048,256]{1,0:T(8,128)(2,1)}, f32[512,1024]{1,0:T(8,128)}) custom-call(s32[1,2]{1,0:T(1,128)} %live.1, bf16[2048,256]{1,0:T(8,128)(2,1)} %win.1, bf16[256,256]{1,0:T(8,128)(2,1)} %bitcast.1, bf16[512,256]{1,0:T(8,128)(2,1)} %pan.1, f32[512,1024]{1,0:T(8,128)} %trail.1), custom_call_target="tpu_custom_call" | custom-call | tf_op jit(solution)/shard_map/fused/pallas_call | solution.py:453
  62.2 2.9 %hand_out.1 = (bf16[512,256]{1,0:T(8,128)(2,1)}, bf16[2048,256]{1,0:T(8,128)(2,1)}, f32[512,1024]{1,0:T(8,128)}) custom-call(bf16[512,256]{1,0:T(8,128)(2,1)} %get-tuple-element.6.pan, bf16[2048,256]{1,0:T(8,128)(2,1)} %get-tuple-element.7.win, f32[512,1024]{1,0:T(8,128)} %get-tuple-element.8.trail), custom_call_target="tpu_custom_call" | custom-call | tf_op jit(solution)/shard_map/hand_out/pallas_call | solution.py:520

commit v4 on v3

--- a/solution.py
+++ b/solution.py
@@ -199,13 +199,11 @@
             if i < 3:
                 part = a_part(k, addr[k] % 8 // n * n, n, g)
                 remote(part, part, ah_send.at[i, g, k], ah_recv.at[i, g, k], near[(k + i) % 4], col).start()
-        if i == 3:
-            for g2 in (2 * g, 2 * g + 1):
-                for k in range(4):
-                    there = slice(k * H, k * H + H), slice(g2 * 2 * B, g2 * 2 * B + 2 * B)
-                    remote(
-                        am.at[there], ao.at[there], a3_send.at[g2, k], a3_recv.at[g2, k], near[(k + 3) % 4], col
-                    ).start()
+
+    def a_last(g):
+        for k in range(4):
+            there = slice(k * H, k * H + H), slice(g * 2 * B, g * 2 * B + 2 * B)
+            remote(fm.at[there], ao.at[there], a3_send.at[g, k], a3_recv.at[g, k], near[(k + 3) % 4], col).start()
 
     pieces = [(1, 0), (2, 0), (3, 1)]
 
@@ -262,11 +260,10 @@
         remote(kp, kept, kr_send, kr_recv, row, (col + d) % 8).start()
     for n in range(len(pieces)):
         whole_send(n)
-    w_step(2)
     a_step(0, 0)
     a_step(0, 1)
+    w_step(2)
     w_step(3)
-
     panel = ar.at[:, lanes(col)]
     local(pv, panel, lsem.at[0]).start()
     for d in range(1, 4):
@@ -275,7 +272,6 @@
 
     a_step(1, 0)
     a_step(1, 1)
-
     take(krow, kr_recv)
 
     @pl.when(own)
@@ -310,13 +306,19 @@
             return raw[at, lane(p)]
         return jnp.concatenate([factors[at, : p * B], raw[at, lane(p)]], axis=1)
 
+    take(kcol.at[0:S, :], kc_recv.at[0])
+    take(kcol.at[S : 2 * S, :], kc_recv.at[1])
+
+    def solve(p, factors, raw):
+        up = u[lane(p), : (p + 1) * B]
+        out = nt(operand(factors, raw, slice(0, 2 * B), p), up)
+        for k in range(4):
+            part = slice(k * H, k * H + H)
+            factors[part, lane(p)] = masked(out[part, :], keep(kcol, k // 2 * S, k % 2, p))
+
     for p in range(N):
         if p == 2:
             whole_take(0)
-        if p == 4:
-            a_step(3, 0)
-        if p == 6:
-            a_step(3, 1)
         if p == 4:
             whole_take(1)
         if p == 6:
@@ -329,22 +331,20 @@
         up = u[lane(p), : (p + 1) * B]
         for q in range(p + 1, N):
             wf[lane(q), lane(p)] = nt(operand(wf, wg, lane(q), p), up).astype(BF)
+        if p == 4:
+            a_step(3, 0)
+        if p == 6:
+            a_step(3, 1)
+        for p2 in ((), (), (), (), (0, 1), (2, 3), (4, 5), (6, 7))[p]:
+            solve(p2, fm, am)
+            if p2 % 2 == 1:
+                a_last(p2 // 2)
 
     here = lanes(col)
     for q in range(N):
         block = wf[lane(q), here]
         wo[lane(q), :] = jnp.where(q > col, block, jnp.zeros_like(block))
     local(wo, win_out, osem.at[0]).start()
-
-    take(kcol.at[0:S, :], kc_recv.at[0])
-    take(kcol.at[S : 2 * S, :], kc_recv.at[1])
-
-    def solve(p, factors, raw):
-        up = u[lane(p), : (p + 1) * B]
-        out = nt(operand(factors, raw, slice(0, 2 * B), p), up)
-        for k in range(4):
-            part = slice(k * H, k * H + H)
-            factors[part, lane(p)] = masked(out[part, :], keep(kcol, k // 2 * S, k % 2, p))
 
     def update(factors, far, first, last):
         for g in range(2):
@@ -359,12 +359,9 @@
                 if last == N * B:
                     local(tr.at[:, at], trail_out.at[:, at], osem.at[2 + 4 * far + k]).start()
 
-    def solve_far(p):
-        if p % 2 == 0:
-            for k in range(4):
-                g = p // 2
-                take(ao.at[k * H : k * H + H, g * 2 * B : g * 2 * B + 2 * B], a3_recv.at[g, k])
-        solve(p, ao, ao)
+    def take_far(g):
+        for k in range(4):
+            take(ao.at[k * H : k * H + H, g * 2 * B : g * 2 * B + 2 * B], a3_recv.at[g, k])
 
     for d in range(1, 4):
         got = ar.at[:, lanes((x + 4 - d) % 4 * 2 + core)]
@@ -373,8 +370,6 @@
     local(pv, panel, lsem.at[0]).wait()
     for d in range(4):
         take(ar.at[:, lanes((x + 4 - d) % 4 * 2 + other)], ad_recv.at[d])
-    for p in range(N):
-        solve(p, fm, am)
     for p in range(N):
         up = u[lane(p), : (p + 1) * B]
         for i in range(2):
@@ -387,14 +382,11 @@
 
     load_trail.wait()
     update(fm, 0, 0, N * B)
-    for p in range(4):
-        solve_far(p)
-
-    solve_far(4)
-    solve_far(5)
+
+    for g in range(3):
+        take_far(g)
     update(ao, 1, 0, 6 * B)
-    solve_far(6)
-    solve_far(7)
+    take_far(3)
     update(ao, 1, 6 * B, N * B)
 
     for j in range(4):
@@ -412,7 +404,7 @@
             for g in range(2):
                 take(a_part(j, addr[j] % 8 // n * n, n, g), ah_send.at[i, g, j])
         for g in range(4):
-            take(am.at[j * H : j * H + H, g * 2 * B : g * 2 * B + 2 * B], a3_send.at[g, j])
+            take(fm.at[j * H : j * H + H, g * 2 * B : g * 2 * B + 2 * B], a3_send.at[g, j])
     take(pv.at[pl.ds(0, 15 * 2 * S), :], a1_send)
     take(pv.at[pl.ds(0, 7 * 4 * S), :], a2_send)
     for n in range(len(pieces)):

time: 65.6 us -> 63.4 us (0.966)
  Pallas kernels: 64.5 us -> 62.6 us
    pallas_call x1, Pallas kernels: 61.6 us -> 59.7 us  [fused(): pl.pallas_call(kernel, out_shape=(jax.ShapeDtypeStruct((2 * B, B), BF), j...]
where the time goes in v4:
time: 63.4 us; the launch traced here: 63.2 us
  Pallas kernels  62.6 us (99%)
  between operations  0.64 us (1%)
    pallas_call x1, Pallas kernels, fused(): pl.pallas_call(kernel, out_shape=(jax.ShapeDtypeStruct((2 * B, B), BF), j...  59.7 us
    pallas_call x1, Pallas kernels, hand_out(): pl.pallas_call(hand_out_kernel, out_shape=tuple((jax.ShapeDtypeStruct(a.s...  2.92 us

profile of v4, /device:TPU:1, one launch (start us, length us, event | category | flops | bytes accessed | tf_op | source)
XLA Modules:
  0.0 63.2 jit_solution(10126394622503556558)
XLA Ops:
  0.6 59.7 %fused.1 = (bf16[512,256]{1,0:T(8,128)(2,1)}, bf16[2048,256]{1,0:T(8,128)(2,1)}, f32[512,1024]{1,0:T(8,128)}) custom-call(s32[1,2]{1,0:T(1,128)} %live.1, bf16[2048,256]{1,0:T(8,128)(2,1)} %win.1, bf16[256,256]{1,0:T(8,128)(2,1)} %bitcast.1, bf16[512,256]{1,0:T(8,128)(2,1)} %pan.1, f32[512,1024]{1,0:T(8,128)} %trail.1), custom_call_target="tpu_custom_call" | custom-call | tf_op jit(solution)/shard_map/fused/pallas_call | solution.py:445
  60.3 2.9 %hand_out.1 = (bf16[512,256]{1,0:T(8,128)(2,1)}, bf16[2048,256]{1,0:T(8,128)(2,1)}, f32[512,1024]{1,0:T(8,128)}) custom-call(bf16[512,256]{1,0:T(8,128)(2,1)} %get-tuple-element.6.pan, bf16[2048,256]{1,0:T(8,128)(2,1)} %get-tuple-element.7.win, f32[512,1024]{1,0:T(8,128)} %get-tuple-element.8.trail), custom_call_target="tpu_custom_call" | custom-call | tf_op jit(solution)/shard_map/hand_out/pallas_call | solution.py:512

commit v5 on v4

--- a/solution.py
+++ b/solution.py
@@ -56,7 +56,7 @@
 
 def kernel(
     live, win, inv, pan, trail, pan_out, win_out, trail_out,
-    pv, pp, st, a0, kp, krow, kcol, iv, wc, wg, wf, u, ar, fr, am, fm, ao, tr, wo, po,
+    pv, pp, st, a0, kp, krow, kf, kcol, iv, wc, wg, wf, u, ar, fr, am, fm, ao, tr, wo, po,
     wx_recv, wx_send, wh_recv, wh_send, wd_recv, wd_send, wr_recv, wr_send, we_recv, we_send,
     a1_recv, a1_send, a2_recv, a2_send, ah_recv, ah_send, a3_recv, a3_send,
     ar_recv, ar_send, ad_recv, ad_send, kr_recv, kr_send, kc_recv, kc_send, lsem, osem,
@@ -125,6 +125,10 @@
 
     lax.fori_loop(1, 16, scatter, 0)
 
+    kept = krow.at[:, pl.ds(pl.multiple_of(col * H, H), H)]
+    local(kp, kept, kr_recv).start()
+    for d in range(1, 8):
+        remote(kp, kept, kr_send, kr_recv, row, (col + d) % 8).start()
     load_window.wait()
     load_inverse.wait()
     wc[lanes(col), :] = iv[...]
@@ -254,14 +258,26 @@
                 remote(src, dst, a2_send, a2_recv.at[x // 2], row, xd * 2 + kc).start()
 
     w_step(1)
-    kept = krow.at[:, pl.ds(pl.multiple_of(col * H, H), H)]
-    local(kp, kept, kr_recv).start()
-    for d in range(1, 8):
-        remote(kp, kept, kr_send, kr_recv, row, (col + d) % 8).start()
+    take(krow, kr_recv)
+    at_row = lax.broadcasted_iota(jnp.int32, (S, H), 0)
+    flags = jnp.zeros((S, H), F32)
+    for p in range(N):
+        two = krow[:, p * H : p * H + H].astype(F32)
+        for i in range(2):
+            flags = jnp.where(at_row == 2 * p + i, two[i : i + 1, :], flags)
+    kf[...] = flags.astype(BF)
+
+    @pl.when(own)
+    def _():
+        dst = kcol.at[rows(h * S, S), :]
+        local(kf, dst, kc_recv.at[h]).start()
+        for d in range(1, 16):
+            remote(kf, dst, kc_send, kc_recv.at[h], (row + d) % 16, col).start()
+
+    a_step(0, 0)
+    a_step(0, 1)
     for n in range(len(pieces)):
         whole_send(n)
-    a_step(0, 0)
-    a_step(0, 1)
     w_step(2)
     w_step(3)
     panel = ar.at[:, lanes(col)]
@@ -272,15 +288,6 @@
 
     a_step(1, 0)
     a_step(1, 1)
-    take(krow, kr_recv)
-
-    @pl.when(own)
-    def _():
-        dst = kcol.at[rows(h * S, S), :]
-        local(krow, dst, kc_recv.at[h]).start()
-        for d in range(1, 16):
-            remote(krow, dst, kc_send, kc_recv.at[h], (row + d) % 16, col).start()
-
     for j in range(4):
         got = w_got(j, 3)
         take(got, wh_recv.at[3, j])
@@ -295,7 +302,7 @@
         take(w_part(j, (1 - a) * 8, 8, other), wd_recv.at[j, 1])
 
     def keep(ref, first, i, p):
-        t = ref[first : first + S, p * H : p * H + H].astype(F32)[i : i + 1, :]
+        t = ref[first : first + S, :].astype(F32)[2 * p + i : 2 * p + i + 1, :]
         return jnp.concatenate([t, t], axis=1) > 0.5
 
     def masked(value, mask):
@@ -373,7 +380,7 @@
     for p in range(N):
         up = u[lane(p), : (p + 1) * B]
         for i in range(2):
-            fr[lane(i), lane(p)] = masked(nt(operand(fr, ar, lane(i), p), up), keep(krow, 0, i, p))
+            fr[lane(i), lane(p)] = masked(nt(operand(fr, ar, lane(i), p), up), keep(kf, 0, i, p))
     f0 = fr[0:B, here]
     f1 = fr[B : 2 * B, here]
     po[0:B, :] = jnp.where(l0 == 0, f0, f1)
@@ -424,7 +431,7 @@
 
     @pl.when(own)
     def _():
-        take(ar.at[0 : 15 * S, 0 : N * H], kc_send)
+        take(ar.at[0:S, 0 : 15 * H], kc_send)
 
     local(wo, win_out, osem.at[0]).wait()
     local(po, pan_out, osem.at[1]).wait()
@@ -458,7 +465,8 @@
             vmem((4 * S, N * B), BF),
             vmem((S, H), BF),
             vmem((S, N * H), BF),
-            vmem((2 * S, N * H), BF),
+            vmem((S, H), BF),
+            vmem((2 * S, H), BF),
             vmem((B, B), BF),
             vmem((N * B, B), BF),
             vmem((N * B, N * B), BF),
@@ -488,7 +496,7 @@
 def hand_out_kernel(pan, win, trail, pan_out, win_out, trail_out, pv, wv, tv, load, store):
     parts = [(pan, pv, pan_out, 0, 512)]
     parts += [(win, wv, win_out, i * 1024, 1024) for i in range(2)]
-    parts += [(trail, tv, trail_out, i * 128, 128) for i in range(4)]
+    parts += [(trail, tv, trail_out, i * 64, 64) for i in range(8)]
 
     def move(n, inward):
         src, mid, dst, first, count = parts[n]
@@ -514,7 +522,7 @@
         out_shape=tuple(jax.ShapeDtypeStruct(a.shape, a.dtype) for a in arrays),
         in_specs=[anys] * 3,
         out_specs=(anys,) * 3,
-        scratch_shapes=[pltpu.VMEM(a.shape, a.dtype) for a in arrays] + [dma((7,)), dma((7,))],
+        scratch_shapes=[pltpu.VMEM(a.shape, a.dtype) for a in arrays] + [dma((11,)), dma((11,))],
         name="hand_out",
     )(*arrays)
 

time: 63.4 us -> 62.3 us (0.983)
  Pallas kernels: 62.6 us -> 61.5 us
    pallas_call x1, Pallas kernels: 59.7 us -> 58.5 us  [fused(): pl.pallas_call(kernel, out_shape=(jax.ShapeDtypeStruct((2 * B, B), BF), j...]
where the time goes in v5:
time: 62.3 us; the launch traced here: 62.1 us
  Pallas kernels  61.5 us (99%)
  between operations  0.64 us (1%)
    pallas_call x1, Pallas kernels, fused(): pl.pallas_call(kernel, out_shape=(jax.ShapeDtypeStruct((2 * B, B), BF), j...  58.5 us
    pallas_call x1, Pallas kernels, hand_out(): pl.pallas_call(hand_out_kernel, out_shape=tuple((jax.ShapeDtypeStruct(a.s...  2.97 us

profile of v5, /device:TPU:1, one launch (start us, length us, event | category | flops | bytes accessed | tf_op | source)
XLA Modules:
  0.0 62.1 jit_solution(18268190226202827726)
XLA Ops:
  0.6 58.5 %fused.1 = (bf16[512,256]{1,0:T(8,128)(2,1)}, bf16[2048,256]{1,0:T(8,128)(2,1)}, f32[512,1024]{1,0:T(8,128)}) custom-call(s32[1,2]{1,0:T(1,128)} %live.1, bf16[2048,256]{1,0:T(8,128)(2,1)} %win.1, bf16[256,256]{1,0:T(8,128)(2,1)} %bitcast.1, bf16[512,256]{1,0:T(8,128)(2,1)} %pan.1, f32[512,1024]{1,0:T(8,128)} %trail.1), custom_call_target="tpu_custom_call" | custom-call | tf_op jit(solution)/shard_map/fused/pallas_call | solution.py:452
  59.2 3.0 %hand_out.1 = (bf16[512,256]{1,0:T(8,128)(2,1)}, bf16[2048,256]{1,0:T(8,128)(2,1)}, f32[512,1024]{1,0:T(8,128)}) custom-call(bf16[512,256]{1,0:T(8,128)(2,1)} %get-tuple-element.6.pan, bf16[2048,256]{1,0:T(8,128)(2,1)} %get-tuple-element.7.win, f32[512,1024]{1,0:T(8,128)} %get-tuple-element.8.trail), custom_call_target="tpu_custom_call" | custom-call | tf_op jit(solution)/shard_map/hand_out/pallas_call | solution.py:520

commit v6 on v5

--- a/solution.py
+++ b/solution.py
@@ -279,6 +279,8 @@
     for n in range(len(pieces)):
         whole_send(n)
     w_step(2)
+    a_step(1, 0)
+    a_step(1, 1)
     w_step(3)
     panel = ar.at[:, lanes(col)]
     local(pv, panel, lsem.at[0]).start()
@@ -286,8 +288,6 @@
         remote(pv, panel, ar_send.at[d - 1], ar_recv.at[d - 1], row, (x + d) % 4 * 2 + core).start()
     remote(pv, panel, ad_send.at[0], ad_recv.at[0], row, sibling).start()
 
-    a_step(1, 0)
-    a_step(1, 1)
     for j in range(4):
         got = w_got(j, 3)
         take(got, wh_recv.at[3, j])

time: 62.3 us -> 61.5 us (0.987)
  Pallas kernels: 61.5 us -> 60.8 us
    pallas_call x1, Pallas kernels: 58.5 us -> 57.8 us  [fused(): pl.pallas_call(kernel, out_shape=(jax.ShapeDtypeStruct((2 * B, B), BF), j...]
where the time goes in v6:
time: 61.5 us; the launch traced here: 61.4 us
  Pallas kernels  60.8 us (99%)
  between operations  0.64 us (1%)
    pallas_call x1, Pallas kernels, fused(): pl.pallas_call(kernel, out_shape=(jax.ShapeDtypeStruct((2 * B, B), BF), j...  57.8 us
    pallas_call x1, Pallas kernels, hand_out(): pl.pallas_call(hand_out_kernel, out_shape=tuple((jax.ShapeDtypeStruct(a.s...  2.97 us

profile of v6, /device:TPU:1, one launch (start us, length us, event | category | flops | bytes accessed | tf_op | source)
XLA Modules:
  0.0 61.4 jit_solution(2441142143998492601)
XLA Ops:
  0.6 57.8 %fused.1 = (bf16[512,256]{1,0:T(8,128)(2,1)}, bf16[2048,256]{1,0:T(8,128)(2,1)}, f32[512,1024]{1,0:T(8,128)}) custom-call(s32[1,2]{1,0:T(1,128)} %live.1, bf16[2048,256]{1,0:T(8,128)(2,1)} %win.1, bf16[256,256]{1,0:T(8,128)(2,1)} %bitcast.1, bf16[512,256]{1,0:T(8,128)(2,1)} %pan.1, f32[512,1024]{1,0:T(8,128)} %trail.1), custom_call_target="tpu_custom_call" | custom-call | tf_op jit(solution)/shard_map/fused/pallas_call | solution.py:452
  58.4 3.0 %hand_out.1 = (bf16[512,256]{1,0:T(8,128)(2,1)}, bf16[2048,256]{1,0:T(8,128)(2,1)}, f32[512,1024]{1,0:T(8,128)}) custom-call(bf16[512,256]{1,0:T(8,128)(2,1)} %get-tuple-element.6.pan, bf16[2048,256]{1,0:T(8,128)(2,1)} %get-tuple-element.7.win, f32[512,1024]{1,0:T(8,128)} %get-tuple-element.8.trail), custom_call_target="tpu_custom_call" | custom-call | tf_op jit(solution)/shard_map/hand_out/pallas_call | solution.py:520
